TPU v7x, 1024 devices: a whole 8x8x8 slice. The times are simulated.
1024 devices in a mesh: head: 2 (over y_lo), inner: 16 (over x, core), outer: 32 (over y_hi, z).
Axes of the slice: x: 8, y: 8 (y_hi: 4, y_lo: 2; y = y_hi * 2 + y_lo), z: 8, core: 2. Of those that a mesh axis runs over, the one named last changes fastest.
Arguments:
- queries: bfloat16 [512, 128, 4096], P(('inner', 'outer'), None, 'head'), may hold values from -2.5 to 2.5
- keys: bfloat16 [512, 128, 512], P(('inner', 'outer'), None, 'head'), may hold values from -2.5 to 2.5
- values: bfloat16 [512, 128, 512], P(('inner', 'outer'), None, 'head'), may hold values from -4 to 4
- grad_out: bfloat16 [512, 128, 4096], P(('inner', 'outer'), None, 'head'), may hold values from -4 to 4
- log_denominator: float32 [512, 128, 32], P(('inner', 'outer'), None, 'head'), may hold values from 6 to 9
- output_row_dot: float32 [512, 128, 32], P(('inner', 'outer'), None, 'head'), may hold values from -32 to 32
- offsets: int32 [512, 2], replicated, may hold values from 0 to 65472, as said below
Outputs:
- grad_query: bfloat16 [512, 128, 4096], P(('inner', 'outer'), 'head')
- grad_key: bfloat16 [512, 128, 512], P(('inner', 'outer'), 'head')
- grad_value: bfloat16 [512, 128, 512], P(('inner', 'outer'), 'head')
Inputs may be any that keep to these rules, and one draw needn't show every extreme that they name: `offsets`: row b holds p * 64 and (1023 - p) * 64, where p runs over a permutation of 0 to 511, so that all blocks' positions together are 0 to 65535, each once.
All inputs are finite; a program needn't handle non-finite values.
Results may differ from a plain program's by a relative error of at most 0.0058.
Values may be sent and summed in bfloat16 or wider, within the bound.
A program may use at most 32 MiB of HBM per device.

v0:
```python
import math

import jax
import jax.numpy as jnp
from jax import lax
from jax.sharding import PartitionSpec as P

HEAD_WIDTH = 128
QUERY_HEADS = 32
KEY_VALUE_HEADS = 4
INNER_STEPS = 3
OUTER_STEPS = 2


def shifted(value, axis, steps):
    count = lax.axis_size(axis)
    pairs = [(source, (source + steps) % count) for source in range(count)]
    return lax.ppermute(value, axis, pairs)


def shift_pairs_inner(stacked, stride):
    return shifted(stacked, "inner", stride)


def shift_pairs_outer(stacked, stride):
    return shifted(stacked, "outer", stride)


def shift_sums_inner(stacked, stride):
    return shifted(stacked, "inner", stride)


def shift_sums_outer(stacked, stride):
    return shifted(stacked, "outer", stride)


def local_positions(offsets, block_index, tokens_per_block):
    halfway = tokens_per_block // 2
    within = jnp.arange(tokens_per_block, dtype=jnp.int32)
    offset_row = lax.dynamic_index_in_dim(offsets, block_index, 0, keepdims=False)
    return jnp.where(within < halfway, offset_row[0], offset_row[1]) + within % halfway


def visit_order():
    visits = []
    for outer_step in range(OUTER_STEPS):
        sweep_order = list(range(INNER_STEPS))
        if outer_step % 2 == 1:
            sweep_order = sweep_order[::-1]
        visits = visits + [(inner_step, outer_step) for inner_step in sweep_order]
    return visits


def pair_terms(
    query_heads, grad_heads, norm_heads, dot_heads, query_pos, key_heads, value_heads, key_pos
):
    scaling = 1.0 / math.sqrt(HEAD_WIDTH)
    scores = (
        jnp.einsum("tgjd,ugd->gjtu", query_heads, key_heads, preferred_element_type=jnp.float32)
        * scaling
    )
    visible = key_pos[None, :] <= query_pos[:, None]
    probabilities = jnp.where(visible, jnp.exp(scores - norm_heads[..., None]), 0.0)
    grad_probs = jnp.einsum(
        "tgjd,ugd->gjtu", grad_heads, value_heads, preferred_element_type=jnp.float32
    )
    grad_scores = probabilities * (grad_probs - dot_heads[..., None])
    probs_low = probabilities.astype(jnp.bfloat16)
    scores_low = grad_scores.astype(jnp.bfloat16)
    grad_value = jnp.einsum(
        "gjtu,tgjd->ugd", probs_low, grad_heads, preferred_element_type=jnp.float32
    )
    grad_key = scaling * jnp.einsum(
        "gjtu,tgjd->ugd", scores_low, query_heads, preferred_element_type=jnp.float32
    )
    grad_query = scaling * jnp.einsum(
        "gjtu,ugd->tgjd", scores_low, key_heads, preferred_element_type=jnp.float32
    )
    tokens_per_block = query_heads.shape[0]
    key_rows = key_heads.shape[0]
    return (
        grad_query.reshape(tokens_per_block, -1),
        grad_key.reshape(key_rows, -1),
        grad_value.reshape(key_rows, -1),
    )


def shards(queries, keys, values, grad_out, log_denominator, output_row_dot, offsets):
    tokens_per_block = queries.shape[1]
    query_cols = queries.shape[2]
    key_value_columns = keys.shape[2]
    heads_kv = key_value_columns // HEAD_WIDTH
    heads_per_group = QUERY_HEADS // KEY_VALUE_HEADS
    query_heads = queries.reshape(tokens_per_block, heads_kv, heads_per_group, HEAD_WIDTH)
    grad_heads = grad_out.reshape(tokens_per_block, heads_kv, heads_per_group, HEAD_WIDTH)
    norm_heads = jnp.transpose(
        log_denominator.reshape(tokens_per_block, heads_kv, heads_per_group), (1, 2, 0)
    )
    dot_heads = jnp.transpose(
        output_row_dot.reshape(tokens_per_block, heads_kv, heads_per_group), (1, 2, 0)
    )
    inner_count = lax.axis_size("inner")
    outer_count = lax.axis_size("outer")
    inner_here = lax.axis_index("inner")
    outer_here = lax.axis_index("outer")
    query_pos = local_positions(offsets, inner_here * outer_count + outer_here, tokens_per_block)
    held_pair = jnp.stack([keys[0], values[0]])
    key_sums = jnp.zeros((2, tokens_per_block, key_value_columns), jnp.float32)
    grad_query = jnp.zeros((tokens_per_block, query_cols), jnp.float32)
    visits = visit_order()
    previous = (0, 0)
    for inner_step, outer_step in visits:
        if inner_step != previous[0]:
            held_pair = shift_pairs_inner(held_pair, inner_step - previous[0])
            key_sums = shift_sums_inner(key_sums, inner_step - previous[0])
        elif outer_step != previous[1]:
            held_pair = shift_pairs_outer(held_pair, outer_step - previous[1])
            key_sums = shift_sums_outer(key_sums, outer_step - previous[1])
        previous = (inner_step, outer_step)
        source = jnp.mod(inner_here - inner_step, inner_count) * outer_count + jnp.mod(
            outer_here - outer_step, outer_count
        )
        key_pos = local_positions(offsets, source, tokens_per_block)
        key_heads = held_pair[0].reshape(tokens_per_block, heads_kv, HEAD_WIDTH)
        value_heads = held_pair[1].reshape(tokens_per_block, heads_kv, HEAD_WIDTH)
        term_query, term_key, term_value = pair_terms(
            query_heads,
            grad_heads,
            norm_heads,
            dot_heads,
            query_pos,
            key_heads,
            value_heads,
            key_pos,
        )
        grad_query = grad_query + term_query
        key_sums = key_sums + jnp.stack([term_key, term_value])
    key_sums = shift_sums_outer(key_sums, -previous[1])
    query_done, key_done, value_done = (
        lax.all_to_all(
            grad_query.astype(jnp.bfloat16), "head", split_axis=0, concat_axis=1, tiled=True
        ),
        lax.all_to_all(
            key_sums[0].astype(jnp.bfloat16), "head", split_axis=0, concat_axis=1, tiled=True
        ),
        lax.all_to_all(
            key_sums[1].astype(jnp.bfloat16), "head", split_axis=0, concat_axis=1, tiled=True
        ),
    )
    return (
        query_done.reshape(1, query_done.shape[0], query_done.shape[1]),
        key_done.reshape(1, key_done.shape[0], key_done.shape[1]),
        value_done.reshape(1, value_done.shape[0], value_done.shape[1]),
    )


def solution(mesh):
    return jax.shard_map(
        shards,
        mesh=mesh,
        in_specs=(
            P(("inner", "outer"), None, "head"),
            P(("inner", "outer"), None, "head"),
            P(("inner", "outer"), None, "head"),
            P(("inner", "outer"), None, "head"),
            P(("inner", "outer"), None, "head"),
            P(("inner", "outer"), None, "head"),
            P(),
        ),
        out_specs=(
            P(("inner", "outer"), "head", None),
            P(("inner", "outer"), "head", None),
            P(("inner", "outer"), "head", None),
        ),
        check_vma=False,
    )
```

profile of v0, /device:TPU:102, one launch (start us, length us, event | category | flops | bytes accessed | tf_op | source)
XLA Modules:
  0.0 128.8 jit_solution(10879770018547447983)
XLA Ops:
  0.7 0.7 copy-done.9
  1.5 0.6 fusion.86
  2.1 0.6 fusion.84
  2.6 0.6 fusion.83
  3.2 0.6 fusion.82
  3.8 0.5 fusion.81
  4.4 0.5 fusion.85
  4.9 0.5 fusion.87
  5.4 1.4 %copy.299 = bf16[1,128,2048]{1,2,0:T(8,128)(2,1)S(1)} copy(bf16[1,128,2048]{2,1,0:T(8,128)(2,1)} %param.7) | data formatting | bytes 1048576 | tf_op jit(solution)/shard_map/reshape | solution.py:94
  7.1 0.6 copy-done.4
  7.7 1.3 select_add_fusion.6
  8.9 2.4 %select_add_fusion.2 = (s32[128]{0:T(128)S(1)}, s32[128]{0:T(128)S(1)}) fusion(s32[]{:T(128)} %bitcast.40, s32[]{:T(128)} %bitcast.39, s32[]{:T(128)} %bitcast.29, s32[]{:T(128)} %bitcast.28), kind=kLoop, calls=%fused_computation.122 | loop fusion | flops 1408 | bytes 1040 | tf_op jit(solution)/shard_map/add | solution.py:41
  11.4 2.5 %select_add_fusion = (s32[128]{0:T(128)S(1)}, s32[128]{0:T(128)S(1)}) fusion(s32[]{:T(128)} %bitcast.62, s32[]{:T(128)} %bitcast.61, s32[]{:T(128)} %bitcast.51, s32[]{:T(128)} %bitcast.50), kind=kLoop, calls=%fused_computation.120 | loop fusion | flops 1408 | bytes 1040 | tf_op jit(solution)/shard_map/add | solution.py:41
  13.9 2.5 %select_add_fusion.4 = (s32[128]{0:T(128)S(1)}, s32[128]{0:T(128)S(1)}) fusion(s32[]{:T(128)} %bitcast.18, s32[]{:T(128)} %bitcast.17, s32[]{:T(128)} %bitcast.3, s32[]{:T(128)} %bitcast.2), kind=kLoop, calls=%fused_computation.124 | loop fusion | flops 1408 | bytes 1040 | tf_op jit(solution)/shard_map/add | solution.py:41
  18.9 0.7 pad_maximum_fusion
  19.9 2.8 %collective-permute-start = (bf16[2,128,256]{1,2,0:T(8,128)(2,1)S(1)}, bf16[2,128,256]{1,2,0:T(8,128)(2,1)S(1)}, u32[]{:S(2)}, u32[]{:S(2)}) collective-permute-start(bf16[2,128,256]{1,2,0:T(8,128)(2,1)S(1)} %pad_maximum_fusion.1), channel_id=1, source_target_pairs={{0,32},{32,64},{64,96},{96,128},{128,160},{160,192},{192,224},{224... | collective-permute-start | bytes 393224 | tf_op jit(solution)/shard_map/ppermute | solution.py:18
  23.1 4.0 %collective-permute-done = bf16[2,128,256]{1,2,0:T(8,128)(2,1)S(1)} collective-permute-done((bf16[2,128,256]{1,2,0:T(8,128)(2,1)S(1)}, bf16[2,128,256]{1,2,0:T(8,128)(2,1)S(1)}, u32[]{:S(2)}, u32[]{:S(2)}) %collective-permute-start) | collective-permute-done | bytes 131104 | tf_op jit(solution)/shard_map/ppermute | solution.py:18
  27.1 0.6 copy-done.7
  29.3 0.8 copy-done.8
  30.8 0.7 maximum_add_fusion
  31.5 3.7 %collective-permute-start.6 = (f32[2,128,256]{2,1,0:T(8,128)}, f32[2,128,256]{2,1,0:T(8,128)}, u32[]{:S(2)}, u32[]{:S(2)}) collective-permute-start(f32[2,128,256]{2,1,0:T(8,128)} %maximum_add_fusion), channel_id=1, source_target_pairs={{0,32},{32,64},{64,96},{96,128},{128,160},{160,192},{192,224},{224... | collective-permute-start | bytes 786440 | tf_op jit(solution)/shard_map/ppermute | solution.py:18
  36.7 5.2 %collective-permute-start.2 = (bf16[2,128,256]{1,2,0:T(8,128)(2,1)S(1)}, bf16[2,128,256]{1,2,0:T(8,128)(2,1)S(1)}, u32[]{:S(2)}, u32[]{:S(2)}) collective-permute-start(bf16[2,128,256]{1,2,0:T(8,128)(2,1)S(1)} %collective-permute-done.1), channel_id=1, source_target_pairs={{0,1},{1,2},{2,3},{3,4},{4,5},{5,6},{6,7},{7,8},{8,9},{9,10},{10,1... | collective-permute-start | bytes 393224 | tf_op jit(solution)/shard_map/ppermute | solution.py:18
  42.4 19.9 %collective-permute-done.2 = bf16[2,128,256]{1,2,0:T(8,128)(2,1)S(1)} collective-permute-done((bf16[2,128,256]{1,2,0:T(8,128)(2,1)S(1)}, bf16[2,128,256]{1,2,0:T(8,128)(2,1)S(1)}, u32[]{:S(2)}, u32[]{:S(2)}) %collective-permute-start.2) | collective-permute-done | bytes 131104 | tf_op jit(solution)/shard_map/ppermute | solution.py:18
  62.3 0.6 copy-done.5
  64.6 0.8 copy-done.6
  65.7 1.7 %maximum_add_fusion.1 = f32[2,128,256]{2,1,0:T(8,128)} fusion(f32[2,128,256]{2,1,0:T(8,128)} %collective-permute-done.6, f32[1,128,256]{2,1,0:T(8,128)S(1)} %copy.199, f32[1,128,256]{2,1,0:T(8,128)S(1)} %copy.198), kind=kLoop, calls=%fused_computation.98 | loop fusion | flops 131072 | bytes 786432 | tf_op jit(solution)/shard_map/add | solution.py:137
  67.4 1.9 %collective-permute-start.7 = (f32[2,128,256]{2,1,0:T(8,128)}, f32[2,128,256]{2,1,0:T(8,128)}, u32[]{:S(2)}, u32[]{:S(2)}) collective-permute-start(f32[2,128,256]{2,1,0:T(8,128)} %maximum_add_fusion.1), channel_id=1, source_target_pairs={{0,1},{1,2},{2,3},{3,4},{4,5},{5,6},{6,7},{7,8},{8,9},{9,10},{10,1... | collective-permute-start | bytes 786440 | tf_op jit(solution)/shard_map/ppermute | solution.py:18
  69.3 0.9 fusion.77
  71.3 1.4 %fusion.19 = f32[128,2,8,128]{3,0,2,1:T(8,128)} fusion(f32[128,2,8,128]{3,0,2,1:T(8,128)S(1)} %fusion.25, bf16[128,2,128,1]{0,2,3,1:T(8,128)(2,1)S(1)} %bitcast.388, bf16[2,8,128,128]{2,3,1,0:T(8,128)(2,1)S(1)} %fusion.49), kind=kOutput, calls=%fused_computation.28 | convolution fusion | flops 67633152 | bytes 2686976 | tf_op jit(solution)/shard_map/gjtu,ugd->tgjd/dot_general | solution.py:76
  73.7 2.3 %collective-permute-done.4 = bf16[2,128,256]{1,2,0:T(8,128)(2,1)S(1)} collective-permute-done((bf16[2,128,256]{1,2,0:T(8,128)(2,1)}, bf16[2,128,256]{1,2,0:T(8,128)(2,1)S(1)}, u32[]{:S(2)}, u32[]{:S(2)}) %collective-permute-start.4) | collective-permute-done | bytes 131104 | tf_op jit(solution)/shard_map/ppermute | solution.py:18
  77.2 9.8 %collective-permute-done.7 = f32[2,128,256]{2,1,0:T(8,128)} collective-permute-done((f32[2,128,256]{2,1,0:T(8,128)}, f32[2,128,256]{2,1,0:T(8,128)}, u32[]{:S(2)}, u32[]{:S(2)}) %collective-permute-start.7) | collective-permute-done | bytes 262176 | tf_op jit(solution)/shard_map/ppermute | solution.py:18
  86.9 1.0 maximum_add_fusion.2
  88.4 3.5 %collective-permute-done.8 = f32[2,128,256]{2,1,0:T(8,128)S(1)} collective-permute-done((f32[2,128,256]{2,1,0:T(8,128)S(1)}, f32[2,128,256]{2,1,0:T(8,128)S(1)}, u32[]{:S(2)}, u32[]{:S(2)}) %collective-permute-start.8) | collective-permute-done | bytes 262176 | tf_op jit(solution)/shard_map/ppermute | solution.py:18
  91.9 1.9 %collective-permute-start.9 = (f32[2,128,256]{2,1,0:T(8,128)S(1)}, f32[2,128,256]{2,1,0:T(8,128)S(1)}, u32[]{:S(2)}, u32[]{:S(2)}) collective-permute-start(f32[2,128,256]{2,1,0:T(8,128)S(1)} %maximum_add_fusion.3), channel_id=1, source_target_pairs={{0,480},{32,0},{64,32},{96,64},{128,96},{160,128},{192,160},{224,1... | collective-permute-start | bytes 786440 | tf_op jit(solution)/shard_map/ppermute | solution.py:18
  93.8 1.6 %fusion.47 = bf16[128,2,8,128]{3,0,2,1:T(8,128)(2,1)S(1)} fusion(f32[128,2,8,128]{3,0,2,1:T(8,128)} %fusion.19, bf16[128,2,128,1]{0,2,3,1:T(8,128)(2,1)S(1)} %bitcast.380, bf16[2,8,128,128]{2,3,1,0:T(8,128)(2,1)S(1)} %fusion.48), kind=kOutput, calls=%fused_computation.65 | convolution fusion | flops 67895296 | bytes 2162688 | tf_op jit(solution)/shard_map/gjtu,ugd->tgjd/dot_general | solution.py:76
  95.7 1.0 reshape.148
  96.7 3.5 %all-to-all-start = ((bf16[2,64,2048]{2,1,0:T(8,128)(2,1)}), bf16[2,64,2048]{2,1,0:T(8,128)(2,1)S(1)}, u32[]{:S(2)}, u32[]{:S(2)}) async-start(bf16[2,64,2048]{2,1,0:T(8,128)(2,1)} %reshape.148), calls=%async_computation | async-start | bytes 1048576 | tf_op jit(solution)/shard_map/all_to_all | solution.py:140
  100.3 1.9 %collective-permute-start.10 = (bf16[2,128,256]{2,1,0:T(8,128)(2,1)S(1)}, bf16[2,128,256]{2,1,0:T(8,128)(2,1)S(1)}, u32[]{:S(2)}, u32[]{:S(2)}) collective-permute-start(bf16[2,128,256]{2,1,0:T(8,128)(2,1)S(1)} %maximum_add_fusion.4), channel_id=1, source_target_pairs={{0,31},{1,0},{2,1},{3,2},{4,3},{5,4},{6,5},{7,6},{8,7},{9,8},{10,9... | collective-permute-start | bytes 393224 | tf_op jit(solution)/shard_map/ppermute | solution.py:18
  102.2 5.9 %collective-permute-done.10 = bf16[2,128,256]{2,1,0:T(8,128)(2,1)S(1)} collective-permute-done((bf16[2,128,256]{2,1,0:T(8,128)(2,1)S(1)}, bf16[2,128,256]{2,1,0:T(8,128)(2,1)S(1)}, u32[]{:S(2)}, u32[]{:S(2)}) %collective-permute-start.10) | collective-permute-done | bytes 131104 | tf_op jit(solution)/shard_map/ppermute | solution.py:18
  108.1 0.6 fusion.75
  108.8 3.7 %all-to-all-done = bf16[2,64,2048]{2,1,0:T(8,128)(2,1)S(1)} async-done(((bf16[2,64,2048]{2,1,0:T(8,128)(2,1)}), bf16[2,64,2048]{2,1,0:T(8,128)(2,1)S(1)}, u32[]{:S(2)}, u32[]{:S(2)}) %all-to-all-start) | async-done | bytes 524320 | tf_op jit(solution)/shard_map/all_to_all | solution.py:140
  112.4 8.2 %all_to_all.39 = bf16[2,64,256]{2,1,0:T(8,128)(2,1)S(1)} all-to-all(bf16[2,64,256]{2,1,0:T(8,128)(2,1)S(1)} %bitcast.421), channel_id=1, replica_groups=mesh['head'=2,'inner'=16,'outer'=32] {'head'}, dimensions={0} | all-to-all | bytes 131072 | tf_op jit(solution)/shard_map/all_to_all | solution.py:143
  120.6 3.3 %all-to-all-start.2 = ((bf16[2,64,256]{2,1,0:T(8,128)(2,1)}), bf16[2,64,256]{2,1,0:T(8,128)(2,1)S(1)}, u32[]{:S(2)}, u32[]{:S(2)}) async-start(bf16[2,64,256]{2,1,0:T(8,128)(2,1)} %bitcast.120), calls=%async_computation.2 | async-start | bytes 131072 | tf_op jit(solution)/shard_map/all_to_all | solution.py:146
  123.9 0.5 copy.181
  124.5 1.2 reshape.142
  125.7 0.7 reshape.143
  126.4 1.6 %all-to-all-done.2 = bf16[2,64,256]{2,1,0:T(8,128)(2,1)S(1)} async-done(((bf16[2,64,256]{2,1,0:T(8,128)(2,1)}), bf16[2,64,256]{2,1,0:T(8,128)(2,1)S(1)}, u32[]{:S(2)}, u32[]{:S(2)}) %all-to-all-start.2) | async-done | bytes 65568 | tf_op jit(solution)/shard_map/all_to_all | solution.py:146
  128.1 0.7 reshape.144
  (81 shorter events, 13.6 us)
Async XLA Ops:
  0.7 0.7 copy-start.9
  5.4 1.4 %copy-start.3 = (bf16[1,128,256]{2,1,0:T(8,128)(2,1)S(1)}, bf16[1,128,256]{2,1,0:T(8,128)(2,1)}, u32[]{:S(2)}) copy-start(bf16[1,128,256]{2,1,0:T(8,128)(2,1)} %param.8) | copy-start | bytes 196612
  5.4 1.4 %copy-start = (bf16[1,128,2048]{2,1,0:T(8,128)(2,1)S(1)}, bf16[1,128,2048]{2,1,0:T(8,128)(2,1)}, u32[]{:S(2)}) copy-start(bf16[1,128,2048]{2,1,0:T(8,128)(2,1)} %param.10) | copy-start | bytes 1572868
  6.8 0.8 copy-start.4
  16.4 0.7 copy-start.1
  17.4 0.7 copy-start.2
  19.7 11.1 %collective-permute-start.5 = (f32[2,128,256]{2,1,0:T(8,128)}, f32[2,128,256]{2,1,0:T(8,128)S(1)}, u32[]{:S(2)}, u32[]{:S(2)}) collective-permute-start(f32[2,128,256]{2,1,0:T(8,128)} %pad_maximum_fusion), channel_id=1, source_target_pairs={{0,32},{32,64},{64,96},{96,128},{128,160},{160,192},{192,224},{224... | collective-permute-start | bytes 786440 | tf_op jit(solution)/shard_map/ppermute | solution.py:18
  19.9 7.1 %collective-permute-start = (bf16[2,128,256]{1,2,0:T(8,128)(2,1)S(1)}, bf16[2,128,256]{1,2,0:T(8,128)(2,1)S(1)}, u32[]{:S(2)}, u32[]{:S(2)}) collective-permute-start(bf16[2,128,256]{1,2,0:T(8,128)(2,1)S(1)} %pad_maximum_fusion.1), channel_id=1, source_target_pairs={{0,32},{32,64},{64,96},{96,128},{128,160},{160,192},{192,224},{224... | collective-permute-start | bytes 393224 | tf_op jit(solution)/shard_map/ppermute | solution.py:18
  27.1 0.6 copy-start.7
  29.2 0.9 copy-start.8
  30.1 5.1 %collective-permute-start.1 = (bf16[2,128,256]{1,2,0:T(8,128)(2,1)S(1)}, bf16[2,128,256]{1,2,0:T(8,128)(2,1)S(1)}, u32[]{:S(2)}, u32[]{:S(2)}) collective-permute-start(bf16[2,128,256]{1,2,0:T(8,128)(2,1)S(1)} %copy-done.8), channel_id=1, source_target_pairs={{0,32},{32,64},{64,96},{96,128},{128,160},{160,192},{192,224},{224... | collective-permute-start | bytes 393224 | tf_op jit(solution)/shard_map/ppermute | solution.py:18
  31.5 34.2 %collective-permute-start.6 = (f32[2,128,256]{2,1,0:T(8,128)}, f32[2,128,256]{2,1,0:T(8,128)}, u32[]{:S(2)}, u32[]{:S(2)}) collective-permute-start(f32[2,128,256]{2,1,0:T(8,128)} %maximum_add_fusion), channel_id=1, source_target_pairs={{0,32},{32,64},{64,96},{96,128},{128,160},{160,192},{192,224},{224... | collective-permute-start | bytes 786440 | tf_op jit(solution)/shard_map/ppermute | solution.py:18
  36.7 25.7 %collective-permute-start.2 = (bf16[2,128,256]{1,2,0:T(8,128)(2,1)S(1)}, bf16[2,128,256]{1,2,0:T(8,128)(2,1)S(1)}, u32[]{:S(2)}, u32[]{:S(2)}) collective-permute-start(bf16[2,128,256]{1,2,0:T(8,128)(2,1)S(1)} %collective-permute-done.1), channel_id=1, source_target_pairs={{0,1},{1,2},{2,3},{3,4},{4,5},{5,6},{6,7},{7,8},{8,9},{9,10},{10,1... | collective-permute-start | bytes 393224 | tf_op jit(solution)/shard_map/ppermute | solution.py:18
  62.3 0.7 copy-start.5
  64.4 0.9 copy-start.6
  65.3 4.0 %collective-permute-start.3 = (bf16[2,128,256]{1,2,0:T(8,128)(2,1)S(1)}, bf16[2,128,256]{1,2,0:T(8,128)(2,1)}, u32[]{:S(2)}, u32[]{:S(2)}) collective-permute-start(bf16[2,128,256]{1,2,0:T(8,128)(2,1)S(1)} %copy-done.6), channel_id=1, source_target_pairs={{0,480},{32,0},{64,32},{96,64},{128,96},{160,128},{192,160},{224,1... | collective-permute-start | bytes 393224 | tf_op jit(solution)/shard_map/ppermute | solution.py:18
  67.4 19.5 %collective-permute-start.7 = (f32[2,128,256]{2,1,0:T(8,128)}, f32[2,128,256]{2,1,0:T(8,128)}, u32[]{:S(2)}, u32[]{:S(2)}) collective-permute-start(f32[2,128,256]{2,1,0:T(8,128)} %maximum_add_fusion.1), channel_id=1, source_target_pairs={{0,1},{1,2},{2,3},{3,4},{4,5},{5,6},{6,7},{7,8},{8,9},{9,10},{10,1... | collective-permute-start | bytes 786440 | tf_op jit(solution)/shard_map/ppermute | solution.py:18
  72.6 3.3 %collective-permute-start.4 = (bf16[2,128,256]{1,2,0:T(8,128)(2,1)}, bf16[2,128,256]{1,2,0:T(8,128)(2,1)S(1)}, u32[]{:S(2)}, u32[]{:S(2)}) collective-permute-start(bf16[2,128,256]{1,2,0:T(8,128)(2,1)} %collective-permute-done.3), channel_id=1, source_target_pairs={{0,480},{32,0},{64,32},{96,64},{128,96},{160,128},{192,160},{224,1... | collective-permute-start | bytes 393224 | tf_op jit(solution)/shard_map/ppermute | solution.py:18
  87.9 3.9 %collective-permute-start.8 = (f32[2,128,256]{2,1,0:T(8,128)S(1)}, f32[2,128,256]{2,1,0:T(8,128)S(1)}, u32[]{:S(2)}, u32[]{:S(2)}) collective-permute-start(f32[2,128,256]{2,1,0:T(8,128)S(1)} %maximum_add_fusion.2), channel_id=1, source_target_pairs={{0,480},{32,0},{64,32},{96,64},{128,96},{160,128},{192,160},{224,1... | collective-permute-start | bytes 786440 | tf_op jit(solution)/shard_map/ppermute | solution.py:18
  91.9 8.4 %collective-permute-start.9 = (f32[2,128,256]{2,1,0:T(8,128)S(1)}, f32[2,128,256]{2,1,0:T(8,128)S(1)}, u32[]{:S(2)}, u32[]{:S(2)}) collective-permute-start(f32[2,128,256]{2,1,0:T(8,128)S(1)} %maximum_add_fusion.3), channel_id=1, source_target_pairs={{0,480},{32,0},{64,32},{96,64},{128,96},{160,128},{192,160},{224,1... | collective-permute-start | bytes 786440 | tf_op jit(solution)/shard_map/ppermute | solution.py:18
  96.7 15.7 %all-to-all-start = ((bf16[2,64,2048]{2,1,0:T(8,128)(2,1)}), bf16[2,64,2048]{2,1,0:T(8,128)(2,1)S(1)}, u32[]{:S(2)}, u32[]{:S(2)}) async-start(bf16[2,64,2048]{2,1,0:T(8,128)(2,1)} %reshape.148), calls=%async_computation | async-start | bytes 1048576 | tf_op jit(solution)/shard_map/all_to_all | solution.py:140
  100.3 7.8 %collective-permute-start.10 = (bf16[2,128,256]{2,1,0:T(8,128)(2,1)S(1)}, bf16[2,128,256]{2,1,0:T(8,128)(2,1)S(1)}, u32[]{:S(2)}, u32[]{:S(2)}) collective-permute-start(bf16[2,128,256]{2,1,0:T(8,128)(2,1)S(1)} %maximum_add_fusion.4), channel_id=1, source_target_pairs={{0,31},{1,0},{2,1},{3,2},{4,3},{5,4},{6,5},{7,6},{8,7},{9,8},{10,9... | collective-permute-start | bytes 393224 | tf_op jit(solution)/shard_map/ppermute | solution.py:18
  120.6 7.4 %all-to-all-start.2 = ((bf16[2,64,256]{2,1,0:T(8,128)(2,1)}), bf16[2,64,256]{2,1,0:T(8,128)(2,1)S(1)}, u32[]{:S(2)}, u32[]{:S(2)}) async-start(bf16[2,64,256]{2,1,0:T(8,128)(2,1)} %bitcast.120), calls=%async_computation.2 | async-start | bytes 131072 | tf_op jit(solution)/shard_map/all_to_all | solution.py:146
where the time goes:
time: 130 us; the launch traced here: 129 us
  waiting for transfers between devices  50.7 us (39%)
  starting transfers between devices  25.1 us (19%)
  local copies, waits for them, and re-layouts  18.2 us (14%)
  other arithmetic  13.1 us (10%)
  matrix products  12.2 us (9%)
  blocking collectives  8.17 us (6%)
  between operations  1.34 us (1%)
    ppermute x11, waiting for transfers between devices, shifted(): return lax.ppermute(value, axis, pairs)  45.4 us
    ppermute x11, starting transfers between devices, shifted(): return lax.ppermute(value, axis, pairs)  18.3 us
    add x4, other arithmetic, local_positions(): jnp.where(within < halfway, offset_row[0], offset_row[1]) + within % halfway  8.68 us
    all_to_all x1, blocking collectives, shards(): lax.all_to_all(key_sums[0].astype(jnp.bfloat16), 'head', split_axis=0, co...  8.17 us
    unnamed x22, local copies, waits for them, and re-layouts  5.24 us
    dot_general x6, matrix products, pair_terms(): jnp.einsum('gjtu,ugd->tgjd', scores_low, key_heads, preferred_element_typ...  4.33 us
    slice x7, local copies, waits for them, and re-layouts, local_positions(): offset_row[0]  3.9 us
    all_to_all x1, waiting for transfers between devices, shards(): lax.all_to_all(grad_query.astype(jnp.bfloat16), 'head', split_axis=0, con...  3.65 us
  transfers between devices with their start and end apart: 13, of which 8 were waited for; matrix products, arithmetic and copies ran while one was open for 16% of the time, Pallas kernels for 0%

commit v1 on v0

v1 whole, which is shorter than its diff:
```python
import functools
import math

import jax
import jax.numpy as jnp
from jax import lax
from jax.experimental import pallas as pl
from jax.experimental.pallas import tpu as pltpu
from jax.sharding import PartitionSpec as P

MESH = pl.DeviceIdType.MESH
F32 = jnp.float32
BF16 = jnp.bfloat16
WIDTH = 128
HALF = 64
GROUPS = 2
SHARED = 8
ROWS = SHARED * HALF
SCALE = 1.0 / math.sqrt(WIDTH)
LOG2E = math.log2(math.e)
HIDDEN = 1.0e5


def product(a, b, dim_a, dim_b):
    return lax.dot_general(
        a, b, (((dim_a,), (dim_b,)), ((), ())), preferred_element_type=F32
    )


def kernel(
    n_inner,
    n_outer,
    q_ref,
    k_ref,
    v_ref,
    do_ref,
    norm_ref,
    dot_ref,
    off_ref,
    oq_ref,
    ok_ref,
    ov_ref,
    q_all,
    do_all,
    q,
    do,
    norm,
    dot,
    dq,
    kv,
    part,
    back,
    got,
    zst,
    zgot,
    hst,
    hgot,
    qst,
    qgot,
    kv_ss,
    kv_rs,
    bk_ss,
    bk_rs,
    z_ss,
    z_rs,
    h_ss,
    h_rs,
    q_ss,
    q_rs,
    in_sem,
):
    i, o, h = lax.axis_index("inner"), lax.axis_index("outer"), lax.axis_index("head")
    other = 1 - h

    def at(di=0, do_=0, head=None):
        return {
            "inner": lax.rem(i + (di + n_inner), n_inner),
            "outer": lax.rem(o + (do_ + n_outer), n_outer),
            "head": h if head is None else head,
        }

    barrier = pltpu.get_barrier_semaphore()
    partners = [at(1), at(-1), at(2), at(-2), at(0, 1), at(0, -1)]
    partners += [at(0, 1, other), at(0, -1, other), at(0, 0, other)]
    for partner in partners:
        pl.semaphore_signal(barrier, inc=1, device_id=partner, device_id_type=MESH)

    loads = []
    for kind, ref in ((0, k_ref), (1, v_ref)):
        for g in range(GROUPS):
            loads.append((ref.at[0, :, pl.ds(g * WIDTH, WIDTH)], kv.at[g, kind, pl.ds(0, WIDTH)]))
    loads += [(q_ref.at[0], q_all), (do_ref.at[0], do_all)]
    loads = [
        pltpu.make_async_copy(source, target, in_sem.at[n])
        for n, (source, target) in enumerate(loads)
    ]
    for load in loads:
        load.start()
    for load in loads[: 2 * GROUPS]:
        load.wait()

    pl.semaphore_wait(barrier, len(partners))

    def slot_copy(source, target, g, device):
        return pltpu.make_async_remote_copy(
            src_ref=kv.at[g, :, pl.ds(source * WIDTH, WIDTH)],
            dst_ref=kv.at[g, :, pl.ds(target * WIDTH, WIDTH)],
            send_sem=kv_ss.at[target - 1, g],
            recv_sem=kv_rs.at[target - 1, g],
            device_id=device,
            device_id_type=MESH,
        )

    def along_outer(g):
        return slot_copy(0, 3, g, at(0, 1))

    def along_inner(row, step, g):
        return slot_copy(3 * row, 3 * row + step, g, at(step))

    def returned(slot, g):
        step = slot % 3
        return pltpu.make_async_remote_copy(
            src_ref=back.at[slot // 3 * 2 + step - 1, g],
            dst_ref=got.at[slot // 3 * 2 + step - 1, g],
            send_sem=bk_ss.at[slot // 3 * 2 + step - 1, g],
            recv_sem=bk_rs.at[slot // 3 * 2 + step - 1, g],
            device_id=at(-step),
            device_id_type=MESH,
        )

    def outer_return(half, g):
        return pltpu.make_async_remote_copy(
            src_ref=zst.at[g, :, pl.ds(half * HALF, HALF)],
            dst_ref=zgot.at[h, g],
            send_sem=z_ss.at[half, g],
            recv_sem=z_rs.at[h, g],
            device_id=at(0, -1, half),
            device_id_type=MESH,
        )

    def outer_arrival(head, g):
        return pltpu.make_async_remote_copy(
            src_ref=zst.at[g, :, pl.ds(0, HALF)],
            dst_ref=zgot.at[head, g],
            send_sem=z_ss.at[0, g],
            recv_sem=z_rs.at[head, g],
            device_id=at(0, -1),
            device_id_type=MESH,
        )

    def head_copy(g):
        return pltpu.make_async_remote_copy(
            src_ref=hst.at[g],
            dst_ref=hgot.at[g],
            send_sem=h_ss.at[g],
            recv_sem=h_rs.at[g],
            device_id=at(0, 0, other),
            device_id_type=MESH,
        )

    def query_copy(g):
        return pltpu.make_async_remote_copy(
            src_ref=qst.at[g],
            dst_ref=qgot.at[g],
            send_sem=q_ss.at[g],
            recv_sem=q_rs.at[g],
            device_id=at(0, 0, other),
            device_id_type=MESH,
        )

    def each_group(body):
        def step(g, carry):
            body(g)
            return carry

        lax.fori_loop(0, GROUPS, step, 0)

    @each_group
    def _(g):
        along_outer(g).start()

    @each_group
    def _(g):
        along_inner(0, 1, g).start()
        along_inner(0, 2, g).start()

    for load in loads[2 * GROUPS :]:
        load.wait()
    for half in range(2):
        rows = slice(half * HALF, (half + 1) * HALF)
        for g in range(GROUPS):
            for j in range(SHARED):
                columns = slice((g * SHARED + j) * WIDTH, (g * SHARED + j + 1) * WIDTH)
                q[half, g, j * HALF : (j + 1) * HALF] = q_all[rows, columns]
                do[half, g, j * HALF : (j + 1) * HALF] = do_all[rows, columns]
    low_lane = lax.broadcasted_iota(jnp.int32, (1, WIDTH), 1) < HALF
    for source, target, factor in ((norm_ref, norm, LOG2E), (dot_ref, dot, 1.0)):
        straight = source[0] * factor
        swapped = pltpu.roll(straight, HALF, 1)
        for g in range(GROUPS):
            for j in range(0, SHARED, 2):
                a, b = g * SHARED + j, g * SHARED + j + 1
                columns = slice(j * HALF, (j + 2) * HALF)
                target[0, g, :, columns] = jnp.where(
                    low_lane, straight[a : a + 1], swapped[b : b + 1]
                )
                target[1, g, :, columns] = jnp.where(
                    low_lane, swapped[a : a + 1], straight[b : b + 1]
                )

    def block_of(slot):
        there = at(-(slot % 3), -(slot // 3))
        return there["inner"] * n_outer + there["outer"]

    def cover(slot, half):
        seen = off_ref[half, block_of(slot)] < off_ref[half, block_of(0)]
        return jnp.where(seen, 0.0, HIDDEN).astype(F32)

    within = lax.broadcasted_iota(jnp.int32, (HALF, ROWS), 0) <= (
        lax.broadcasted_iota(jnp.int32, (HALF, ROWS), 1) % HALF
    )

    def tile(half, g, keys, values, slots, kinds):
        queries, grads = q[half, g], do[half, g]
        bias = norm[half, g]
        scores = product(keys, queries, 1, 1) * (SCALE * LOG2E)
        pieces = []
        for n, (slot, key_half) in enumerate(kinds):
            piece = scores[n * HALF : (n + 1) * HALF]
            if key_half != half:
                piece = jnp.exp2(piece - bias)
            elif slot == 0:
                piece = jnp.where(within, jnp.exp2(piece - bias), 0.0)
            else:
                piece = jnp.exp2(piece - (bias + cover(slot, half)))
            pieces.append(piece)
        probs = jnp.concatenate(pieces, 0)
        grad_probs = product(values, grads, 1, 1)
        grad_scores = (probs * (grad_probs - dot[half, g])).astype(BF16)
        probs = probs.astype(BF16)
        grad_value = product(probs, grads, 1, 0)
        grad_key = product(grad_scores, queries, 1, 0)
        term = product(grad_scores, keys, 0, 0)
        dq[half, g] = term if slots[0] == 0 else dq[half, g] + term
        return grad_key, grad_value

    def compute(slots, g):
        here = pl.ds(slots[0] * WIDTH, len(slots) * WIDTH)
        keys, values = kv[g, 0, here], kv[g, 1, here]
        count = range(len(slots))
        early = lambda x: jnp.concatenate([x[n * WIDTH : n * WIDTH + HALF] for n in count], 0)
        late_side = tile(1, g, keys, values, slots, [(s, kh) for s in slots for kh in (0, 1)])
        early_side = tile(0, g, early(keys), early(values), slots, [(s, 0) for s in slots])
        sums = []
        for n in count:
            both = []
            for a, b in zip(late_side, early_side):
                low = a[n * WIDTH : n * WIDTH + HALF] + b[n * HALF : (n + 1) * HALF]
                both.append((low, a[n * WIDTH + HALF : (n + 1) * WIDTH]))
            sums.append(both)
        return sums

    def put(ref, lead, pair):
        for kind, factor in ((0, SCALE), (1, 1.0)):
            for half in range(2):
                rows = slice(half * HALF, (half + 1) * HALF)
                ref[(*lead, kind, rows)] = (pair[kind][half] * factor).astype(ref.dtype)

    def pair_of_slots(row, g):
        one, two = compute((3 * row + 1, 3 * row + 2), g)
        put(back, (2 * row + 1, g), two)
        returned(3 * row + 2, g).start()
        put(back, (2 * row, g), one)
        returned(3 * row + 1, g).start()

    @each_group
    def _(g):
        put(part, (0, g), compute((0,), g)[0])

    @each_group
    def _(g):
        along_inner(0, 1, g).wait_recv()
        along_inner(0, 2, g).wait_recv()
        pair_of_slots(0, g)
        along_outer(g).wait_recv()
        along_inner(1, 1, g).start()
        along_inner(1, 2, g).start()

    @each_group
    def _(g):
        put(part, (1, g), compute((3,), g)[0])

    def collect(row, g):
        returned(3 * row + 1, g).wait_recv()
        returned(3 * row + 2, g).wait_recv()
        return part[row, g] + got[2 * row, g].astype(F32) + got[2 * row + 1, g].astype(F32)

    @each_group
    def _(g):
        part[0, g] = collect(0, g)
        hst[g] = part[0, g, :, pl.ds(other * HALF, HALF)].astype(BF16)
        head_copy(g).start()

    @each_group
    def _(g):
        along_inner(1, 1, g).wait_recv()
        along_inner(1, 2, g).wait_recv()
        pair_of_slots(1, g)
        first = h * (GROUPS * SHARED * WIDTH) + g * (SHARED * WIDTH)
        for j in range(SHARED):
            rows = slice(j * HALF, (j + 1) * HALF)
            qst[g, :, j * WIDTH : (j + 1) * WIDTH] = (dq[other, g, rows] * SCALE).astype(BF16)
        query_copy(g).start()
        for j in range(SHARED):
            rows = slice(j * HALF, (j + 1) * HALF)
            columns = pl.ds(pl.multiple_of(first + j * WIDTH, WIDTH), WIDTH)
            oq_ref[0, :, columns] = (dq[h, g, rows] * SCALE).astype(BF16)

    @each_group
    def _(g):
        zst[g] = collect(1, g).astype(BF16)
        outer_return(0, g).start()
        outer_return(1, g).start()

    @each_group
    def _(g):
        query_copy(g).wait_recv()
        first = other * (GROUPS * SHARED * WIDTH) + g * (SHARED * WIDTH)
        columns = pl.ds(pl.multiple_of(first, WIDTH), SHARED * WIDTH)
        oq_ref[0, :, columns] = qgot[g]

    @each_group
    def _(g):
        mine = pl.ds(pl.multiple_of(h * (GROUPS * WIDTH) + g * WIDTH, WIDTH), WIDTH)
        theirs = pl.ds(pl.multiple_of(other * (GROUPS * WIDTH) + g * WIDTH, WIDTH), WIDTH)
        head_copy(g).wait_recv()
        outer_arrival(0, g).wait_recv()
        outer_arrival(1, g).wait_recv()
        for kind, ref in ((0, ok_ref), (1, ov_ref)):
            own = part[0, g, kind, pl.ds(h * HALF, HALF)] + zgot[h, g, kind].astype(F32)
            ref[0, :, mine] = own.astype(BF16)
            far = hgot[g, kind].astype(F32) + zgot[other, g, kind].astype(F32)
            ref[0, :, theirs] = far.astype(BF16)

    @each_group
    def _(g):
        along_outer(g).wait_send()
        for row in range(2):
            for step in (1, 2):
                along_inner(row, step, g).wait_send()
                returned(3 * row + step, g).wait_send()
        head_copy(g).wait_send()
        query_copy(g).wait_send()
        outer_return(0, g).wait_send()
        outer_return(1, g).wait_send()


def solution(mesh):
    n_inner, n_outer = mesh.shape["inner"], mesh.shape["outer"]
    vmem = pl.BlockSpec(memory_space=pltpu.VMEM)
    hbm = pl.BlockSpec(memory_space=pltpu.HBM)
    square = (2, WIDTH, WIDTH)
    part_half = (2, HALF, WIDTH)
    dma = pltpu.SemaphoreType.DMA

    def shards(queries, keys, values, grad_out, log_denominator, row_dot, offsets):
        columns = GROUPS * SHARED * WIDTH
        return pl.pallas_call(
            functools.partial(kernel, n_inner, n_outer),
            out_shape=[
                jax.ShapeDtypeStruct((1, HALF, 2 * columns), BF16),
                jax.ShapeDtypeStruct((1, HALF, 2 * GROUPS * WIDTH), BF16),
                jax.ShapeDtypeStruct((1, HALF, 2 * GROUPS * WIDTH), BF16),
            ],
            in_specs=[hbm] * 4 + [vmem] * 2 + [pl.BlockSpec(memory_space=pltpu.SMEM)],
            out_specs=[vmem] * 3,
            scratch_shapes=[
                pltpu.VMEM((WIDTH, columns), BF16),
                pltpu.VMEM((WIDTH, columns), BF16),
                pltpu.VMEM((2, GROUPS, ROWS, WIDTH), BF16),
                pltpu.VMEM((2, GROUPS, ROWS, WIDTH), BF16),
                pltpu.VMEM((2, GROUPS, 1, ROWS), F32),
                pltpu.VMEM((2, GROUPS, 1, ROWS), F32),
                pltpu.VMEM((2, GROUPS, ROWS, WIDTH), F32),
                pltpu.VMEM((GROUPS, 2, 6 * WIDTH, WIDTH), BF16),
                pltpu.VMEM((2, GROUPS, *square), F32),
                pltpu.VMEM((4, GROUPS, *square), BF16),
                pltpu.VMEM((4, GROUPS, *square), BF16),
                pltpu.VMEM((GROUPS, *square), BF16),
                pltpu.VMEM((2, GROUPS, *part_half), BF16),
                pltpu.VMEM((GROUPS, *part_half), BF16),
                pltpu.VMEM((GROUPS, *part_half), BF16),
                pltpu.VMEM((GROUPS, HALF, SHARED * WIDTH), BF16),
                pltpu.VMEM((GROUPS, HALF, SHARED * WIDTH), BF16),
                dma((5, GROUPS)),
                dma((5, GROUPS)),
                dma((4, GROUPS)),
                dma((4, GROUPS)),
                dma((2, GROUPS)),
                dma((2, GROUPS)),
                dma((GROUPS,)),
                dma((GROUPS,)),
                dma((GROUPS,)),
                dma((GROUPS,)),
                dma((2 * GROUPS + 2,)),
            ],
            compiler_params=pltpu.CompilerParams(
                collective_id=0, has_side_effects=True, vmem_limit_bytes=60 << 20
            ),
        )(
            queries,
            keys,
            values,
            grad_out,
            jnp.swapaxes(log_denominator, 1, 2),
            jnp.swapaxes(row_dot, 1, 2),
            offsets.T,
        )

    spec_in = P(("inner", "outer"), None, "head")
    spec_out = P(("inner", "outer"), "head", None)
    return jax.shard_map(
        shards,
        mesh=mesh,
        in_specs=(spec_in,) * 6 + (P(),),
        out_specs=(spec_out,) * 3,
        check_vma=False,
    )
```

time: 130 us -> 52.3 us (0.40)
  the two profiles are of different devices: /device:TPU:102 before, /device:TPU:21 now
where the time goes in v1:
time: 52.3 us; the launch traced here: 52 us
  Pallas kernels  48 us (92%)
  local copies, waits for them, and re-layouts  3.4 us (7%)
  between operations  0.65 us (1%)
    pallas_call x1, Pallas kernels, shards(): pl.pallas_call(functools.partial(kernel, n_inner, n_outer), out_shape=[ja...  48 us
    unnamed x7, local copies, waits for them, and re-layouts  3.4 us

profile of v1, /device:TPU:21, one launch (start us, length us, event | category | flops | bytes accessed | tf_op | source)
XLA Modules:
  0.0 52.0 jit_solution(8476100000759974141)
XLA Ops:
  0.6 48.0 %shard_map.94 = (bf16[1,64,4096]{2,1,0:T(8,128)(2,1)}, bf16[1,64,512]{2,1,0:T(8,128)(2,1)}, bf16[1,64,512]{2,1,0:T(8,128)(2,1)}) custom-call(bf16[1,128,2048]{2,1,0:T(8,128)(2,1)} %q_ref.1, bf16[1,128,256]{2,1,0:T(8,128)(2,1)} %k_ref.1, bf16[1,128,256]{2,1,0:T(8,128)(2,1)} %v_ref.1, bf16[1,128,2048]{2,1,0:T(8,128)(2,1)} %do_ref.1, f32[1,16,128]{2,1,0:T(8,128)} %bitcast.3, ...), custom_call_target="tpu_custom_call" | custom-call | tf_op jit(solution)/shard_map/pallas_call | solution.py:368
  48.6 0.0 copy-start.1
  48.6 1.9 %copy.13 = bf16[1,64,4096]{2,1,0:T(8,128)(2,1)} copy(bf16[1,64,4096]{2,1,0:T(8,128)(2,1)} %get-tuple-element.6) | data formatting | bytes 1048576
  50.5 0.0 copy-done.1
  50.5 0.0 copy-start
  50.5 0.6 %copy.14 = bf16[1,64,512]{2,1,0:T(8,128)(2,1)} copy(bf16[1,64,512]{2,1,0:T(8,128)(2,1)S(1)} %copy-done.1) | data formatting | bytes 131072
  51.1 0.2 copy-done
  51.4 0.6 %copy.15 = bf16[1,64,512]{2,1,0:T(8,128)(2,1)} copy(bf16[1,64,512]{2,1,0:T(8,128)(2,1)S(1)} %copy-done) | data formatting | bytes 131072
Async XLA Ops:
  48.6 1.9 %copy-start.1 = (bf16[1,64,512]{2,1,0:T(8,128)(2,1)S(1)}, bf16[1,64,512]{2,1,0:T(8,128)(2,1)}, u32[]{:S(2)}) copy-start(bf16[1,64,512]{2,1,0:T(8,128)(2,1)} %get-tuple-element.7) | copy-start | bytes 196612
  50.5 0.9 %copy-start = (bf16[1,64,512]{2,1,0:T(8,128)(2,1)S(1)}, bf16[1,64,512]{2,1,0:T(8,128)(2,1)}, u32[]{:S(2)}) copy-start(bf16[1,64,512]{2,1,0:T(8,128)(2,1)} %get-tuple-element.8) | copy-start | bytes 196612

commit v2 on v1

--- a/solution.py
+++ b/solution.py
@@ -18,6 +18,7 @@
 ROWS = SHARED * HALF
 SCALE = 1.0 / math.sqrt(WIDTH)
 LOG2E = math.log2(math.e)
+DEPTH = 8
 HIDDEN = 1.0e5
 
 
@@ -52,6 +53,7 @@
     back,
     got,
     zst,
+    relay,
     zgot,
     hst,
     hgot,
@@ -67,6 +69,9 @@
     h_rs,
     q_ss,
     q_rs,
+    r_ss,
+    r_rs,
+    f_ss,
     in_sem,
 ):
     i, o, h = lax.axis_index("inner"), lax.axis_index("outer"), lax.axis_index("head")
@@ -78,12 +83,6 @@
             "outer": lax.rem(o + (do_ + n_outer), n_outer),
             "head": h if head is None else head,
         }
-
-    barrier = pltpu.get_barrier_semaphore()
-    partners = [at(1), at(-1), at(2), at(-2), at(0, 1), at(0, -1)]
-    partners += [at(0, 1, other), at(0, -1, other), at(0, 0, other)]
-    for partner in partners:
-        pl.semaphore_signal(barrier, inc=1, device_id=partner, device_id_type=MESH)
 
     loads = []
     for kind, ref in ((0, k_ref), (1, v_ref)):
@@ -96,10 +95,34 @@
     ]
     for load in loads:
         load.start()
+
+    barrier = pltpu.get_barrier_semaphore()
+    partners = [at(1), at(-1), at(2), at(-2), at(0, 1), at(0, -1)]
+    partners += [at(0, 1, other), at(0, -1, other), at(0, 0, other)]
+    place = lax.rem(o, DEPTH)
+    first_of_row, last_of_row = place == 0, place == DEPTH - 1
+    relays_first = [at(0, DEPTH - 1)]
+    relays_last = [at(0, 1 - DEPTH)] + [at(0, d, side) for d in (-DEPTH, DEPTH) for side in (0, 1)]
+
+    def greet(devices):
+        for device in devices:
+            pl.semaphore_signal(barrier, inc=1, device_id=device, device_id_type=MESH)
+
+    greet(partners)
+
+    @pl.when(first_of_row)
+    def _():
+        greet(relays_first)
+
+    @pl.when(last_of_row)
+    def _():
+        greet(relays_last)
+
     for load in loads[: 2 * GROUPS]:
         load.wait()
 
-    pl.semaphore_wait(barrier, len(partners))
+    more = jnp.where(first_of_row, len(relays_first), 0) + jnp.where(last_of_row, len(relays_last), 0)
+    pl.semaphore_wait(barrier, len(partners) + more)
 
     def slot_copy(source, target, g, device):
         return pltpu.make_async_remote_copy(
@@ -148,6 +171,26 @@
             device_id_type=MESH,
         )
 
+    def relay_copy(g):
+        return pltpu.make_async_remote_copy(
+            src_ref=zst.at[g],
+            dst_ref=relay.at[g],
+            send_sem=r_ss.at[g],
+            recv_sem=r_rs.at[g],
+            device_id=at(0, DEPTH - 1),
+            device_id_type=MESH,
+        )
+
+    def relay_onward(half, g):
+        return pltpu.make_async_remote_copy(
+            src_ref=relay.at[g, :, pl.ds(half * HALF, HALF)],
+            dst_ref=zgot.at[h, g],
+            send_sem=f_ss.at[half, g],
+            recv_sem=z_rs.at[h, g],
+            device_id=at(0, -DEPTH, half),
+            device_id_type=MESH,
+        )
+
     def head_copy(g):
         return pltpu.make_async_remote_copy(
             src_ref=hst.at[g],
@@ -175,14 +218,12 @@
 
         lax.fori_loop(0, GROUPS, step, 0)
 
-    @each_group
-    def _(g):
-        along_outer(g).start()
-
-    @each_group
-    def _(g):
+    along_outer(0).start()
+
+    @each_group
+    def _(g):
+        along_inner(0, 2, g).start()
         along_inner(0, 1, g).start()
-        along_inner(0, 2, g).start()
 
     for load in loads[2 * GROUPS :]:
         load.wait()
@@ -273,6 +314,9 @@
         put(back, (2 * row, g), one)
         returned(3 * row + 1, g).start()
 
+    along_outer(0).wait_send()
+    along_outer(1).start()
+
     @each_group
     def _(g):
         put(part, (0, g), compute((0,), g)[0])
@@ -282,9 +326,12 @@
         along_inner(0, 1, g).wait_recv()
         along_inner(0, 2, g).wait_recv()
         pair_of_slots(0, g)
+
+    @each_group
+    def _(g):
         along_outer(g).wait_recv()
+        along_inner(1, 2, g).start()
         along_inner(1, 1, g).start()
-        along_inner(1, 2, g).start()
 
     @each_group
     def _(g):
@@ -319,8 +366,15 @@
     @each_group
     def _(g):
         zst[g] = collect(1, g).astype(BF16)
-        outer_return(0, g).start()
-        outer_return(1, g).start()
+
+        @pl.when(first_of_row)
+        def _():
+            relay_copy(g).start()
+
+        @pl.when(jnp.logical_not(first_of_row))
+        def _():
+            outer_return(0, g).start()
+            outer_return(1, g).start()
 
     @each_group
     def _(g):
@@ -328,6 +382,14 @@
         first = other * (GROUPS * SHARED * WIDTH) + g * (SHARED * WIDTH)
         columns = pl.ds(pl.multiple_of(first, WIDTH), SHARED * WIDTH)
         oq_ref[0, :, columns] = qgot[g]
+
+    @pl.when(last_of_row)
+    def _():
+        @each_group
+        def _(g):
+            relay_copy(g).wait_recv()
+            relay_onward(0, g).start()
+            relay_onward(1, g).start()
 
     @each_group
     def _(g):
@@ -342,17 +404,41 @@
             far = hgot[g, kind].astype(F32) + zgot[other, g, kind].astype(F32)
             ref[0, :, theirs] = far.astype(BF16)
 
-    @each_group
-    def _(g):
-        along_outer(g).wait_send()
+    along_outer(1).wait_send()
+
+    @each_group
+    def _(g):
         for row in range(2):
             for step in (1, 2):
                 along_inner(row, step, g).wait_send()
                 returned(3 * row + step, g).wait_send()
         head_copy(g).wait_send()
         query_copy(g).wait_send()
-        outer_return(0, g).wait_send()
-        outer_return(1, g).wait_send()
+
+        @pl.when(first_of_row)
+        def _():
+            relay_copy(g).wait_send()
+
+        @pl.when(jnp.logical_not(first_of_row))
+        def _():
+            outer_return(0, g).wait_send()
+            outer_return(1, g).wait_send()
+
+        @pl.when(last_of_row)
+        def _():
+            relay_onward(0, g).wait_send()
+            relay_onward(1, g).wait_send()
+
+
+def place_kernel(*refs):
+    count = (len(refs) - 1) // 2
+    copies = [
+        pltpu.make_async_copy(refs[n], refs[count + n], refs[-1].at[n]) for n in range(count)
+    ]
+    for copy in copies:
+        copy.start()
+    for copy in copies:
+        copy.wait()
 
 
 def solution(mesh):
@@ -365,13 +451,14 @@
 
     def shards(queries, keys, values, grad_out, log_denominator, row_dot, offsets):
         columns = GROUPS * SHARED * WIDTH
-        return pl.pallas_call(
+        shapes = [
+            jax.ShapeDtypeStruct((1, HALF, 2 * columns), BF16),
+            jax.ShapeDtypeStruct((1, HALF, 2 * GROUPS * WIDTH), BF16),
+            jax.ShapeDtypeStruct((1, HALF, 2 * GROUPS * WIDTH), BF16),
+        ]
+        sums = pl.pallas_call(
             functools.partial(kernel, n_inner, n_outer),
-            out_shape=[
-                jax.ShapeDtypeStruct((1, HALF, 2 * columns), BF16),
-                jax.ShapeDtypeStruct((1, HALF, 2 * GROUPS * WIDTH), BF16),
-                jax.ShapeDtypeStruct((1, HALF, 2 * GROUPS * WIDTH), BF16),
-            ],
+            out_shape=[pltpu.VMEM(shape.shape, shape.dtype) for shape in shapes],
             in_specs=[hbm] * 4 + [vmem] * 2 + [pl.BlockSpec(memory_space=pltpu.SMEM)],
             out_specs=[vmem] * 3,
             scratch_shapes=[
@@ -386,6 +473,7 @@
                 pltpu.VMEM((2, GROUPS, *square), F32),
                 pltpu.VMEM((4, GROUPS, *square), BF16),
                 pltpu.VMEM((4, GROUPS, *square), BF16),
+                pltpu.VMEM((GROUPS, *square), BF16),
                 pltpu.VMEM((GROUPS, *square), BF16),
                 pltpu.VMEM((2, GROUPS, *part_half), BF16),
                 pltpu.VMEM((GROUPS, *part_half), BF16),
@@ -402,10 +490,13 @@
                 dma((GROUPS,)),
                 dma((GROUPS,)),
                 dma((GROUPS,)),
+                dma((GROUPS,)),
+                dma((GROUPS,)),
+                dma((2, GROUPS)),
                 dma((2 * GROUPS + 2,)),
             ],
             compiler_params=pltpu.CompilerParams(
-                collective_id=0, has_side_effects=True, vmem_limit_bytes=60 << 20
+                collective_id=0, has_side_effects=True, vmem_limit_bytes=56 << 20
             ),
         )(
             queries,
@@ -416,6 +507,14 @@
             jnp.swapaxes(row_dot, 1, 2),
             offsets.T,
         )
+        return pl.pallas_call(
+            place_kernel,
+            out_shape=shapes,
+            in_specs=[vmem] * 3,
+            out_specs=[pl.BlockSpec(memory_space=pl.ANY)] * 3,
+            scratch_shapes=[dma((3,))],
+            compiler_params=pltpu.CompilerParams(vmem_limit_bytes=4 << 20),
+        )(*sums)
 
     spec_in = P(("inner", "outer"), None, "head")
     spec_out = P(("inner", "outer"), "head", None)

time: 52.3 us -> 45.2 us (0.86)
  the two profiles are of different devices: /device:TPU:21 before, /device:TPU:6 now
where the time goes in v2:
time: 45.2 us; the launch traced here: 44.6 us
  Pallas kernels  44 us (97%)
  between operations  0.64 us (1%)
    pallas_call x1, Pallas kernels, shards(): pl.pallas_call(functools.partial(kernel, n_inner, n_outer), out_shape=[pl...  43.1 us

profile of v2, /device:TPU:6, one launch (start us, length us, event | category | flops | bytes accessed | tf_op | source)
XLA Modules:
  0.0 44.6 jit_solution(6332968451318420095)
XLA Ops:
  0.6 43.1 %shard_map.94 = (bf16[1,64,4096]{2,1,0:T(8,128)(2,1)S(1)}, bf16[1,64,512]{2,1,0:T(8,128)(2,1)S(1)}, bf16[1,64,512]{2,1,0:T(8,128)(2,1)S(1)}) custom-call(bf16[1,128,2048]{2,1,0:T(8,128)(2,1)} %q_ref.1, bf16[1,128,256]{2,1,0:T(8,128)(2,1)} %k_ref.1, bf16[1,128,256]{2,1,0:T(8,128)(2,1)} %v_ref.1, bf16[1,128,2048]{2,1,0:T(8,128)(2,1)} %do_ref.1, ...), custom_call_target="tpu_custom_call" | custom-call | tf_op jit(solution)/shard_map/pallas_call | solution.py:459
  43.8 0.9 %shard_map.95 = (bf16[1,64,4096]{2,1,0:T(8,128)(2,1)}, bf16[1,64,512]{2,1,0:T(8,128)(2,1)}, bf16[1,64,512]{2,1,0:T(8,128)(2,1)}) custom-call(bf16[1,64,4096]{2,1,0:T(8,128)(2,1)S(1)} %get-tuple-element.6.refs_0_, bf16[1,64,512]{2,1,0:T(8,128)(2,1)S(1)} %get-tuple-element.7.refs_1_, bf16[1,64,512]{2,1,0:T(8,128)(2,1)S(1)} %get-tuple-element.8.refs_2_), custom_call_target="tpu_custom_call" | custom-call | tf_op jit(solution)/shard_map/pallas_call | solution.py:510

commit v3 on v2

--- a/solution.py
+++ b/solution.py
@@ -72,6 +72,7 @@
     r_ss,
     r_rs,
     f_ss,
+    ready,
     in_sem,
 ):
     i, o, h = lax.axis_index("inner"), lax.axis_index("outer"), lax.axis_index("head")
@@ -97,32 +98,33 @@
         load.start()
 
     barrier = pltpu.get_barrier_semaphore()
-    partners = [at(1), at(-1), at(2), at(-2), at(0, 1), at(0, -1)]
-    partners += [at(0, 1, other), at(0, -1, other), at(0, 0, other)]
     place = lax.rem(o, DEPTH)
     first_of_row, last_of_row = place == 0, place == DEPTH - 1
-    relays_first = [at(0, DEPTH - 1)]
-    relays_last = [at(0, 1 - DEPTH)] + [at(0, d, side) for d in (-DEPTH, DEPTH) for side in (0, 1)]
+    not_first, not_last = jnp.logical_not(first_of_row), jnp.logical_not(last_of_row)
 
     def greet(devices):
         for device in devices:
             pl.semaphore_signal(barrier, inc=1, device_id=device, device_id_type=MESH)
 
-    greet(partners)
+    greet([at(0, -1), at(0, 0, other), at(1), at(-1), at(2), at(-2)])
+
+    @pl.when(not_last)
+    def _():
+        greet([at(0, 1), at(0, 1, other)])
 
     @pl.when(first_of_row)
     def _():
-        greet(relays_first)
+        greet([at(0, DEPTH - 1)])
 
     @pl.when(last_of_row)
     def _():
-        greet(relays_last)
+        greet([at(0, DEPTH, 0), at(0, DEPTH, 1)])
 
     for load in loads[: 2 * GROUPS]:
         load.wait()
 
-    more = jnp.where(first_of_row, len(relays_first), 0) + jnp.where(last_of_row, len(relays_last), 0)
-    pl.semaphore_wait(barrier, len(partners) + more)
+    greeted = 6 + jnp.where(not_first, 2, 0) + jnp.where(last_of_row, 3, 0)
+    pl.semaphore_wait(barrier, greeted)
 
     def slot_copy(source, target, g, device):
         return pltpu.make_async_remote_copy(
@@ -219,6 +221,12 @@
         lax.fori_loop(0, GROUPS, step, 0)
 
     along_outer(0).start()
+
+    @pl.when(last_of_row)
+    def _():
+        pl.semaphore_signal(
+            ready, inc=1, device_id=at(0, 1 - DEPTH), device_id_type=MESH
+        )
 
     @each_group
     def _(g):
@@ -332,9 +340,6 @@
         along_outer(g).wait_recv()
         along_inner(1, 2, g).start()
         along_inner(1, 1, g).start()
-
-    @each_group
-    def _(g):
         put(part, (1, g), compute((3,), g)[0])
 
     def collect(row, g):
@@ -363,6 +368,10 @@
             columns = pl.ds(pl.multiple_of(first + j * WIDTH, WIDTH), WIDTH)
             oq_ref[0, :, columns] = (dq[h, g, rows] * SCALE).astype(BF16)
 
+    @pl.when(first_of_row)
+    def _():
+        pl.semaphore_wait(ready, 1)
+
     @each_group
     def _(g):
         zst[g] = collect(1, g).astype(BF16)
@@ -371,7 +380,7 @@
         def _():
             relay_copy(g).start()
 
-        @pl.when(jnp.logical_not(first_of_row))
+        @pl.when(not_first)
         def _():
             outer_return(0, g).start()
             outer_return(1, g).start()
@@ -419,7 +428,7 @@
         def _():
             relay_copy(g).wait_send()
 
-        @pl.when(jnp.logical_not(first_of_row))
+        @pl.when(not_first)
         def _():
             outer_return(0, g).wait_send()
             outer_return(1, g).wait_send()
@@ -493,6 +502,7 @@
                 dma((GROUPS,)),
                 dma((GROUPS,)),
                 dma((2, GROUPS)),
+                pltpu.SemaphoreType.REGULAR,
                 dma((2 * GROUPS + 2,)),
             ],
             compiler_params=pltpu.CompilerParams(

time: 45.2 us -> 43.8 us (0.969)
  Pallas kernels: 44 us -> 42.9 us
    pallas_call x1, Pallas kernels: 43.1 us -> 42 us  [shards(): pl.pallas_call(functools.partial(kernel, n_inner, n_outer), out_shape=[pl...]
where the time goes in v3:
time: 43.8 us; the launch traced here: 43.5 us
  Pallas kernels  42.9 us (98%)
  between operations  0.64 us (1%)
    pallas_call x1, Pallas kernels, shards(): pl.pallas_call(functools.partial(kernel, n_inner, n_outer), out_shape=[pl...  42 us

profile of v3, /device:TPU:6, one launch (start us, length us, event | category | flops | bytes accessed | tf_op | source)
XLA Modules:
  0.0 43.5 jit_solution(568684735642874163)
XLA Ops:
  0.6 42.0 %shard_map.94 = (bf16[1,64,4096]{2,1,0:T(8,128)(2,1)S(1)}, bf16[1,64,512]{2,1,0:T(8,128)(2,1)S(1)}, bf16[1,64,512]{2,1,0:T(8,128)(2,1)S(1)}) custom-call(bf16[1,128,2048]{2,1,0:T(8,128)(2,1)} %q_ref.1, bf16[1,128,256]{2,1,0:T(8,128)(2,1)} %k_ref.1, bf16[1,128,256]{2,1,0:T(8,128)(2,1)} %v_ref.1, bf16[1,128,2048]{2,1,0:T(8,128)(2,1)} %do_ref.1, ...), custom_call_target="tpu_custom_call" | custom-call | tf_op jit(solution)/shard_map/pallas_call | solution.py:468
  42.6 0.9 %shard_map.95 = (bf16[1,64,4096]{2,1,0:T(8,128)(2,1)}, bf16[1,64,512]{2,1,0:T(8,128)(2,1)}, bf16[1,64,512]{2,1,0:T(8,128)(2,1)}) custom-call(bf16[1,64,4096]{2,1,0:T(8,128)(2,1)S(1)} %get-tuple-element.6.refs_0_, bf16[1,64,512]{2,1,0:T(8,128)(2,1)S(1)} %get-tuple-element.7.refs_1_, bf16[1,64,512]{2,1,0:T(8,128)(2,1)S(1)} %get-tuple-element.8.refs_2_), custom_call_target="tpu_custom_call" | custom-call | tf_op jit(solution)/shard_map/pallas_call | solution.py:520

commit v4 on v3

--- a/solution.py
+++ b/solution.py
@@ -54,6 +54,7 @@
     got,
     zst,
     relay,
+    zrel,
     zgot,
     hst,
     hgot,
@@ -114,7 +115,7 @@
 
     @pl.when(first_of_row)
     def _():
-        greet([at(0, DEPTH - 1)])
+        greet([at(-step, DEPTH - 1) for step in range(3)])
 
     @pl.when(last_of_row)
     def _():
@@ -123,7 +124,7 @@
     for load in loads[: 2 * GROUPS]:
         load.wait()
 
-    greeted = 6 + jnp.where(not_first, 2, 0) + jnp.where(last_of_row, 3, 0)
+    greeted = 6 + jnp.where(not_first, 2, 0) + jnp.where(last_of_row, 5, 0)
     pl.semaphore_wait(barrier, greeted)
 
     def slot_copy(source, target, g, device):
@@ -173,19 +174,19 @@
             device_id_type=MESH,
         )
 
-    def relay_copy(g):
-        return pltpu.make_async_remote_copy(
-            src_ref=zst.at[g],
-            dst_ref=relay.at[g],
-            send_sem=r_ss.at[g],
-            recv_sem=r_rs.at[g],
-            device_id=at(0, DEPTH - 1),
+    def relay_copy(step, g):
+        return pltpu.make_async_remote_copy(
+            src_ref=back.at[1 + step, g] if step else zst.at[g],
+            dst_ref=relay.at[step, g],
+            send_sem=r_ss.at[step, g],
+            recv_sem=r_rs.at[step, g],
+            device_id=at(-step, DEPTH - 1),
             device_id_type=MESH,
         )
 
     def relay_onward(half, g):
         return pltpu.make_async_remote_copy(
-            src_ref=relay.at[g, :, pl.ds(half * HALF, HALF)],
+            src_ref=zrel.at[g, :, pl.ds(half * HALF, HALF)],
             dst_ref=zgot.at[h, g],
             send_sem=f_ss.at[half, g],
             recv_sem=z_rs.at[h, g],
@@ -224,9 +225,9 @@
 
     @pl.when(last_of_row)
     def _():
-        pl.semaphore_signal(
-            ready, inc=1, device_id=at(0, 1 - DEPTH), device_id_type=MESH
-        )
+        for step in range(3):
+            first = at(step, 1 - DEPTH)
+            pl.semaphore_signal(ready, inc=1, device_id=first, device_id_type=MESH)
 
     @each_group
     def _(g):
@@ -318,9 +319,21 @@
     def pair_of_slots(row, g):
         one, two = compute((3 * row + 1, 3 * row + 2), g)
         put(back, (2 * row + 1, g), two)
-        returned(3 * row + 2, g).start()
         put(back, (2 * row, g), one)
-        returned(3 * row + 1, g).start()
+        if row == 0:
+            returned(2, g).start()
+            returned(1, g).start()
+            return
+
+        @pl.when(not_first)
+        def _():
+            returned(5, g).start()
+            returned(4, g).start()
+
+        @pl.when(first_of_row)
+        def _():
+            relay_copy(2, g).start()
+            relay_copy(1, g).start()
 
     along_outer(0).wait_send()
     along_outer(1).start()
@@ -334,6 +347,10 @@
         along_inner(0, 1, g).wait_recv()
         along_inner(0, 2, g).wait_recv()
         pair_of_slots(0, g)
+
+    @pl.when(first_of_row)
+    def _():
+        pl.semaphore_wait(ready, 3)
 
     @each_group
     def _(g):
@@ -341,6 +358,11 @@
         along_inner(1, 2, g).start()
         along_inner(1, 1, g).start()
         put(part, (1, g), compute((3,), g)[0])
+
+        @pl.when(first_of_row)
+        def _():
+            zst[g] = part[1, g].astype(BF16)
+            relay_copy(0, g).start()
 
     def collect(row, g):
         returned(3 * row + 1, g).wait_recv()
@@ -368,20 +390,11 @@
             columns = pl.ds(pl.multiple_of(first + j * WIDTH, WIDTH), WIDTH)
             oq_ref[0, :, columns] = (dq[h, g, rows] * SCALE).astype(BF16)
 
-    @pl.when(first_of_row)
-    def _():
-        pl.semaphore_wait(ready, 1)
-
-    @each_group
-    def _(g):
-        zst[g] = collect(1, g).astype(BF16)
-
-        @pl.when(first_of_row)
-        def _():
-            relay_copy(g).start()
-
-        @pl.when(not_first)
-        def _():
+    @pl.when(not_first)
+    def _():
+        @each_group
+        def _(g):
+            zst[g] = collect(1, g).astype(BF16)
             outer_return(0, g).start()
             outer_return(1, g).start()
 
@@ -396,7 +409,9 @@
     def _():
         @each_group
         def _(g):
-            relay_copy(g).wait_recv()
+            for step in range(3):
+                relay_copy(step, g).wait_recv()
+            zrel[g] = sum(relay[step, g].astype(F32) for step in range(3)).astype(BF16)
             relay_onward(0, g).start()
             relay_onward(1, g).start()
 
@@ -417,19 +432,22 @@
 
     @each_group
     def _(g):
-        for row in range(2):
-            for step in (1, 2):
-                along_inner(row, step, g).wait_send()
-                returned(3 * row + step, g).wait_send()
+        for step in (1, 2):
+            along_inner(0, step, g).wait_send()
+            along_inner(1, step, g).wait_send()
+            returned(step, g).wait_send()
         head_copy(g).wait_send()
         query_copy(g).wait_send()
 
         @pl.when(first_of_row)
         def _():
-            relay_copy(g).wait_send()
+            for step in range(3):
+                relay_copy(step, g).wait_send()
 
         @pl.when(not_first)
         def _():
+            returned(4, g).wait_send()
+            returned(5, g).wait_send()
             outer_return(0, g).wait_send()
             outer_return(1, g).wait_send()
 
@@ -483,6 +501,7 @@
                 pltpu.VMEM((4, GROUPS, *square), BF16),
                 pltpu.VMEM((4, GROUPS, *square), BF16),
                 pltpu.VMEM((GROUPS, *square), BF16),
+                pltpu.VMEM((3, GROUPS, *square), BF16),
                 pltpu.VMEM((GROUPS, *square), BF16),
                 pltpu.VMEM((2, GROUPS, *part_half), BF16),
                 pltpu.VMEM((GROUPS, *part_half), BF16),
@@ -499,8 +518,8 @@
                 dma((GROUPS,)),
                 dma((GROUPS,)),
                 dma((GROUPS,)),
-                dma((GROUPS,)),
-                dma((GROUPS,)),
+                dma((3, GROUPS)),
+                dma((3, GROUPS)),
                 dma((2, GROUPS)),
                 pltpu.SemaphoreType.REGULAR,
                 dma((2 * GROUPS + 2,)),

time: 43.8 us -> 41.7 us (0.952)
  Pallas kernels: 42.9 us -> 40.9 us
    pallas_call x1, Pallas kernels: 42 us -> 40 us  [shards(): pl.pallas_call(functools.partial(kernel, n_inner, n_outer), out_shape=[pl...]
where the time goes in v4:
time: 41.7 us; the launch traced here: 41.5 us
  Pallas kernels  40.9 us (98%)
  between operations  0.64 us (2%)
    pallas_call x1, Pallas kernels, shards(): pl.pallas_call(functools.partial(kernel, n_inner, n_outer), out_shape=[pl...  40 us
    pallas_call x1, Pallas kernels, shards(): pl.pallas_call(place_kernel, out_shape=shapes, in_specs=[vmem] * 3, out_s...  0.85 us

profile of v4, /device:TPU:6, one launch (start us, length us, event | category | flops | bytes accessed | tf_op | source)
XLA Modules:
  0.0 41.5 jit_solution(3895208030792121975)
XLA Ops:
  0.6 40.0 %shard_map.94 = (bf16[1,64,4096]{2,1,0:T(8,128)(2,1)S(1)}, bf16[1,64,512]{2,1,0:T(8,128)(2,1)S(1)}, bf16[1,64,512]{2,1,0:T(8,128)(2,1)S(1)}) custom-call(bf16[1,128,2048]{2,1,0:T(8,128)(2,1)} %q_ref.1, bf16[1,128,256]{2,1,0:T(8,128)(2,1)} %k_ref.1, bf16[1,128,256]{2,1,0:T(8,128)(2,1)} %v_ref.1, bf16[1,128,2048]{2,1,0:T(8,128)(2,1)} %do_ref.1, ...), custom_call_target="tpu_custom_call" | custom-call | tf_op jit(solution)/shard_map/pallas_call | solution.py:486
  40.6 0.9 %shard_map.95 = (bf16[1,64,4096]{2,1,0:T(8,128)(2,1)}, bf16[1,64,512]{2,1,0:T(8,128)(2,1)}, bf16[1,64,512]{2,1,0:T(8,128)(2,1)}) custom-call(bf16[1,64,4096]{2,1,0:T(8,128)(2,1)S(1)} %get-tuple-element.6.refs_0_, bf16[1,64,512]{2,1,0:T(8,128)(2,1)S(1)} %get-tuple-element.7.refs_1_, bf16[1,64,512]{2,1,0:T(8,128)(2,1)S(1)} %get-tuple-element.8.refs_2_), custom_call_target="tpu_custom_call" | custom-call | tf_op jit(solution)/shard_map/pallas_call | solution.py:539

commit v5 on v4

--- a/solution.py
+++ b/solution.py
@@ -107,7 +107,7 @@
         for device in devices:
             pl.semaphore_signal(barrier, inc=1, device_id=device, device_id_type=MESH)
 
-    greet([at(0, -1), at(0, 0, other), at(1), at(-1), at(2), at(-2)])
+    greet([at(0, -1), at(0, 0, other), at(-1), at(-2)])
 
     @pl.when(not_last)
     def _():
@@ -124,7 +124,7 @@
     for load in loads[: 2 * GROUPS]:
         load.wait()
 
-    greeted = 6 + jnp.where(not_first, 2, 0) + jnp.where(last_of_row, 5, 0)
+    greeted = 4 + jnp.where(not_first, 2, 0) + jnp.where(last_of_row, 5, 0)
     pl.semaphore_wait(barrier, greeted)
 
     def slot_copy(source, target, g, device):
@@ -316,8 +316,15 @@
                 rows = slice(half * HALF, (half + 1) * HALF)
                 ref[(*lead, kind, rows)] = (pair[kind][half] * factor).astype(ref.dtype)
 
-    def pair_of_slots(row, g):
+    def send_queries(g):
+        for j in range(SHARED):
+            rows = slice(j * HALF, (j + 1) * HALF)
+            qst[g, :, j * WIDTH : (j + 1) * WIDTH] = (dq[other, g, rows] * SCALE).astype(BF16)
+        query_copy(g).start()
+
+    def pair_of_slots(row, g, first=lambda g: None):
         one, two = compute((3 * row + 1, 3 * row + 2), g)
+        first(g)
         put(back, (2 * row + 1, g), two)
         put(back, (2 * row, g), one)
         if row == 0:
@@ -379,16 +386,7 @@
     def _(g):
         along_inner(1, 1, g).wait_recv()
         along_inner(1, 2, g).wait_recv()
-        pair_of_slots(1, g)
-        first = h * (GROUPS * SHARED * WIDTH) + g * (SHARED * WIDTH)
-        for j in range(SHARED):
-            rows = slice(j * HALF, (j + 1) * HALF)
-            qst[g, :, j * WIDTH : (j + 1) * WIDTH] = (dq[other, g, rows] * SCALE).astype(BF16)
-        query_copy(g).start()
-        for j in range(SHARED):
-            rows = slice(j * HALF, (j + 1) * HALF)
-            columns = pl.ds(pl.multiple_of(first + j * WIDTH, WIDTH), WIDTH)
-            oq_ref[0, :, columns] = (dq[h, g, rows] * SCALE).astype(BF16)
+        pair_of_slots(1, g, send_queries)
 
     @pl.when(not_first)
     def _():
@@ -397,6 +395,14 @@
             zst[g] = collect(1, g).astype(BF16)
             outer_return(0, g).start()
             outer_return(1, g).start()
+
+    @each_group
+    def _(g):
+        first = h * (GROUPS * SHARED * WIDTH) + g * (SHARED * WIDTH)
+        for j in range(SHARED):
+            rows = slice(j * HALF, (j + 1) * HALF)
+            columns = pl.ds(pl.multiple_of(first + j * WIDTH, WIDTH), WIDTH)
+            oq_ref[0, :, columns] = (dq[h, g, rows] * SCALE).astype(BF16)
 
     @each_group
     def _(g):

time: 41.7 us -> 41.7 us (level)
  no operation moved by 1% of the time
where the time goes in v5:
time: 41.7 us; the launch traced here: 41.5 us
  Pallas kernels  40.8 us (98%)
  between operations  0.64 us (2%)
    pallas_call x1, Pallas kernels, shards(): pl.pallas_call(functools.partial(kernel, n_inner, n_outer), out_shape=[pl...  40 us
    pallas_call x1, Pallas kernels, shards(): pl.pallas_call(place_kernel, out_shape=shapes, in_specs=[vmem] * 3, out_s...  0.85 us

profile of v5, /device:TPU:6, one launch (start us, length us, event | category | flops | bytes accessed | tf_op | source)
XLA Modules:
  0.0 41.5 jit_solution(10025789888322318977)
XLA Ops:
  0.6 40.0 %shard_map.94 = (bf16[1,64,4096]{2,1,0:T(8,128)(2,1)S(1)}, bf16[1,64,512]{2,1,0:T(8,128)(2,1)S(1)}, bf16[1,64,512]{2,1,0:T(8,128)(2,1)S(1)}) custom-call(bf16[1,128,2048]{2,1,0:T(8,128)(2,1)} %q_ref.1, bf16[1,128,256]{2,1,0:T(8,128)(2,1)} %k_ref.1, bf16[1,128,256]{2,1,0:T(8,128)(2,1)} %v_ref.1, bf16[1,128,2048]{2,1,0:T(8,128)(2,1)} %do_ref.1, ...), custom_call_target="tpu_custom_call" | custom-call | tf_op jit(solution)/shard_map/pallas_call | solution.py:492
  40.6 0.9 %shard_map.95 = (bf16[1,64,4096]{2,1,0:T(8,128)(2,1)}, bf16[1,64,512]{2,1,0:T(8,128)(2,1)}, bf16[1,64,512]{2,1,0:T(8,128)(2,1)}) custom-call(bf16[1,64,4096]{2,1,0:T(8,128)(2,1)S(1)} %get-tuple-element.6.refs_0_, bf16[1,64,512]{2,1,0:T(8,128)(2,1)S(1)} %get-tuple-element.7.refs_1_, bf16[1,64,512]{2,1,0:T(8,128)(2,1)S(1)} %get-tuple-element.8.refs_2_), custom_call_target="tpu_custom_call" | custom-call | tf_op jit(solution)/shard_map/pallas_call | solution.py:545
